TPU v7x, 128 devices: a whole 4x4x4 slice. The times are simulated.
128 devices in a mesh: rows: 32 (over z, x, core), cols: 4 (over y).
Axes of the slice: x: 4, y: 4, z: 4, core: 2. Of those that a mesh axis runs over, the one named last changes fastest.
Arguments:
- panel_cols: float32 [262144, 256], P(('rows', 'cols')), may hold values from -10000 to 10000, as said below
- trailing: float32 [262144, 1024], P('rows', 'cols'), may hold values from -200000 to 200000
Outputs:
- r_factor: float32 [256, 256], replicated
- r_cross: float32 [256, 1024], P(None, 'cols')
- updated: float32 [262144, 1024], P('rows', 'cols')
Inputs may be any that keep to these rules, and one draw needn't show every extreme that they name: panel_cols has full column rank.
All inputs are finite; a program needn't handle non-finite values.
Results may differ from a plain program's by a relative error of at most 0.0003.
Values sent between devices are 32-bit elements; how exact they have to be, the bound alone decides.
No kernel may reach another device: no remote copies, remote signals or barrier semaphores. Data moves between devices by JAX's collectives and lax.ppermute only.
A program may use at most 128 MiB of HBM per device.

v0:
```python
import math
import jax
import jax.numpy as jnp
from jax import lax
from jax.sharding import PartitionSpec as P


def matmul(left, right):
    return jnp.dot(left, right, precision=lax.Precision.HIGHEST)


def lower_factor(gram_sum):
    return jnp.linalg.cholesky(gram_sum)


def lower_inverse(lower):
    identity = jnp.eye(lower.shape[0], dtype=jnp.float32)
    return jax.scipy.linalg.solve_triangular(lower, identity, lower=True)


def local(panel_cols, trailing):
    rows_total = trailing.shape[0] * lax.axis_size("rows")
    shrink = 1.0 / math.sqrt(rows_total)
    gram_sum = lax.psum(matmul(panel_cols.T, panel_cols), ("rows", "cols"))
    lower = lower_factor(gram_sum)
    inverse = lower_inverse(lower)
    basis_part = matmul(panel_cols, inverse.T)
    orthonormal = lax.all_gather(basis_part, "cols", axis=0, tiled=True)
    coupling = lax.psum(matmul(orthonormal.T, trailing), "rows")
    updated = trailing - matmul(orthonormal, coupling)
    return (lower.T * shrink, coupling * shrink, updated)


def solution(mesh):
    in_specs = (P(("rows", "cols"), None), P("rows", "cols"))
    out_specs = (P(), P(None, "cols"), P("rows", "cols"))
    return jax.shard_map(local, mesh=mesh, in_specs=in_specs, out_specs=out_specs, check_vma=False)
```

profile of v0, /device:TPU:1, one launch (start us, length us, event | category | flops | bytes accessed | tf_op | source)
XLA Modules:
  0.0 447.2 jit_solution(1440533770498955808)
XLA Ops:
  7.2 1.5 copy-done
  8.8 4.2 fusion.14
  13.2 145.0 %all-reduce.4.cloned.1.call-done = f32[256,256]{0,1:T(8,128)} async-done(((f32[256,256]{0,1:T(8,128)}), f32[256,256]{0,1:T(8,128)}) %all-reduce.4.cloned.1.call-update) | async-done | bytes 262160 | tf_op jit(solution)/shard_map/psum | solution.py:24
  158.2 1.1 copy.6
  159.3 1.0 fusion.3
  160.3 11.7 %cholesky.50 = f32[128,128]{1,0:T(8,128)S(1)} custom-call(f32[128,128]{1,0:T(8,128)S(1)} %cholesky.118), custom_call_target="Cholesky" | custom-call | tf_op jit(solution)/shard_map/jit(cholesky)/cholesky | solution.py:13
  172.0 9.8 %custom-call.15 = f32[1,128,128]{1,2,0:T(8,128)S(1)} custom-call(f32[1,128,128]{2,1,0:T(8,128)S(1)} %get-tuple-element.29), custom_call_target="InvertDiagBlocksLowerTriangular" | custom-call | tf_op jit(solution)/shard_map/jit(cholesky)/cholesky | solution.py:13
  182.1 0.3 convolution_subtract_fusion.2
  182.3 11.7 %cholesky.105 = f32[128,128]{1,0:T(8,128)S(1)} custom-call(f32[128,128]{1,0:T(8,128)S(1)} %convolution_subtract_fusion.2), custom_call_target="Cholesky" | custom-call | tf_op jit(solution)/shard_map/jit(cholesky)/cholesky | solution.py:13
  194.1 0.6 compare_reduce_fusion
  196.2 4.2 while.1
  196.3 0.6 fusion.28
  196.9 1.4 bitcast_dynamic-update-slice_fusion.2
  198.3 0.6 fusion.28
  198.9 1.4 bitcast_dynamic-update-slice_fusion.2
  200.3 19.7 %custom-call.16 = f32[2,128,128]{1,2,0:T(8,128)S(1)} custom-call(f32[2,128,128]{2,1,0:T(8,128)S(1)} %get-tuple-element.10), custom_call_target="InvertDiagBlocksLowerTriangular" | custom-call | tf_op jit(solution)/shard_map/jit(_solve_triangular)/triangular_solve | solution.py:18
  220.6 0.3 fusion.8
  220.9 3.3 convolution_bitcast_fusion
  224.2 80.6 %all-gather.2.cloned.1.call-done = f32[8192,256]{0,1:T(8,128)} async-done(((f32[2048,256]{0,1:T(8,128)}), f32[8192,256]{0,1:T(8,128)}) %all-gather.2.cloned.1.call-update) | async-done | bytes 8388624 | tf_op jit(solution)/shard_map/all_gather | solution.py:28
  304.8 11.4 %fusion.15 = f32[256,256]{1,0:T(8,128)} fusion(f32[8192,256]{0,1:T(8,128)} %all-gather.2.cloned.1.call-done, f32[8192,256]{1,0:T(8,128)} %param.3), kind=kOutput, calls=%fused_computation.39 | convolution fusion | flops 6442450944 | bytes 17039360 | tf_op jit(solution)/shard_map/dot_general | solution.py:9
  316.2 0.8 copy.7
  317.1 101.8 %all-reduce.6.cloned.1.call-done = f32[256,256]{1,0:T(8,128)} async-done(((f32[256,256]{1,0:T(8,128)}), f32[256,256]{1,0:T(8,128)}) %all-reduce.6.cloned.1.call-update) | async-done | bytes 262160 | tf_op jit(solution)/shard_map/psum | solution.py:29
  418.9 21.1 %convolution_subtract_fusion = f32[8192,256]{1,0:T(8,128)} fusion(f32[8192,256]{1,0:T(8,128)} %param.3, f32[8192,256]{0,1:T(8,128)} %all-gather.2.cloned.1.call-done, f32[256,256]{1,0:T(8,128)} %all-reduce.6.cloned.1.call-done), kind=kOutput, calls=%fused_computation.2 | convolution fusion | flops 6444548096 | bytes 25427968 | tf_op jit(solution)/shard_map/dot_general | solution.py:9
  440.0 0.7 broadcast_multiply_fusion
  (23 shorter events, 1.3 us)
Async XLA Ops:
  7.2 1.6 copy-start
  7.2 151.0 %all-reduce.4.cloned.1.call-start = ((), (), s32[]{:S(2)}) async-start(), calls=%async_computation | async-start | bytes 524288 | tf_op jit(solution)/shard_map/psum | solution.py:24
  12.9 291.9 %all-gather.2.cloned.1.call-start = ((), (), s32[]{:S(2)}) async-start(), calls=%async_computation.1 | async-start | bytes 10485760 | tf_op jit(solution)/shard_map/all_gather | solution.py:28
  224.2 194.7 %all-reduce.6.cloned.1.call-start = ((), (), s32[]{:S(2)}) async-start(), calls=%async_computation.2 | async-start | bytes 524288 | tf_op jit(solution)/shard_map/psum | solution.py:29
  418.9 21.1 %copy-start.1 = (f32[256,256]{1,0:T(8,128)S(1)}, f32[256,256]{1,0:T(8,128)}, u32[]{:S(2)}) copy-start(f32[256,256]{1,0:T(8,128)} %all-reduce.6.cloned.1.call-done) | copy-start | bytes 786436
Sparse Core Ops, SparseCore 0:
  13.3 144.8 all-reduce.3
  224.3 80.4 all-gather.1
  316.4 102.4 all-reduce.5
where the time goes:
time: 447 us
  waiting for transfers between devices  327 us (73%)
  other arithmetic  55.4 us (12%)
  matrix products  41.2 us (9%)
  between operations  15.2 us (3%)
  local copies, waits for them, and re-layouts  7.51 us (2%)
    psum x1, waiting for transfers between devices, local(): gram_sum = lax.psum(matmul(panel_cols.T, panel_cols), ('rows', 'cols'))  145 us
    psum x1, waiting for transfers between devices, local(): coupling = lax.psum(matmul(orthonormal.T, trailing), 'rows')  102 us
    all_gather x1, waiting for transfers between devices, local(): orthonormal = lax.all_gather(basis_part, 'cols', axis=0, tiled=True)  80.6 us
    dot_general x4, matrix products, matmul(): return jnp.dot(left, right, precision=lax.Precision.HIGHEST)  39.9 us
    another operation x6, other arithmetic, lower_factor(): return jnp.linalg.cholesky(gram_sum)  34 us
    another operation x3, other arithmetic, lower_inverse(): return jax.scipy.linalg.solve_triangular(lower, identity, lower=True)  19.7 us
  transfers between devices with their start and end apart: 3, of which 3 were waited for; matrix products, arithmetic and copies ran while one was open for 0% of the time, Pallas kernels for 0%

commit v1 on v0

--- a/solution.py
+++ b/solution.py
@@ -25,7 +25,9 @@
     lower = lower_factor(gram_sum)
     inverse = lower_inverse(lower)
     basis_part = matmul(panel_cols, inverse.T)
-    orthonormal = lax.all_gather(basis_part, "cols", axis=0, tiled=True)
+    orthonormal = jnp.concatenate(
+        lax.all_to_all(jnp.stack([basis_part] * lax.axis_size("cols")), "cols", 0, 0), axis=0
+    )
     coupling = lax.psum(matmul(orthonormal.T, trailing), "rows")
     updated = trailing - matmul(orthonormal, coupling)
     return (lower.T * shrink, coupling * shrink, updated)

time: 447 us -> 482 us (1.078)
  blocking collectives: 0 us -> 96.6 us
  waiting for transfers between devices: 327 us -> 244 us
  loops' own time: 0.21 us -> 12.4 us
  local copies, waits for them, and re-layouts: 7.51 us -> 16.1 us
    all_to_all x0 -> x1, blocking collectives: none -> 96.6 us  [local(): lax.all_to_all(jnp.stack([basis_part] * lax.axis_size('cols')), 'cols', 0...]
    all_gather x1 -> x0, waiting for transfers between devices: 80.6 us -> none  [local(): orthonormal = lax.all_gather(basis_part, 'cols', axis=0, tiled=True)]
    another operation x1, loops' own time: 0.21 us -> 12.4 us  [lower_inverse(): return jax.scipy.linalg.solve_triangular(lower, identity, lower=True)]
  transfers between devices with their start and end apart: 3 -> 2, of which waited for: 3 -> 2; matrix products, arithmetic and copies ran while one was open for 0% -> 0% of each run, Pallas kernels for 0% -> 0%
where the time goes in v1:
time: 482 us; the launch traced here: 478 us
  waiting for transfers between devices  244 us (51%)
  blocking collectives  96.6 us (20%)
  other arithmetic  55.4 us (11%)
  matrix products  37.9 us (8%)
  local copies, waits for them, and re-layouts  16.1 us (3%)
  between operations  15.7 us (3%)
  loops' own time  12.4 us (3%)
    psum x1, waiting for transfers between devices, local(): gram_sum = lax.psum(matmul(panel_cols.T, panel_cols), ('rows', 'cols'))  145 us
    psum x1, waiting for transfers between devices, local(): coupling = lax.psum(matmul(orthonormal.T, trailing), 'rows')  98.9 us
    all_to_all x1, blocking collectives, local(): lax.all_to_all(jnp.stack([basis_part] * lax.axis_size('cols')), 'cols', 0...  96.6 us
    dot_general x4, matrix products, matmul(): return jnp.dot(left, right, precision=lax.Precision.HIGHEST)  36.6 us
    another operation x6, other arithmetic, lower_factor(): return jnp.linalg.cholesky(gram_sum)  34 us
    another operation x3, other arithmetic, lower_inverse(): return jax.scipy.linalg.solve_triangular(lower, identity, lower=True)  19.7 us
    another operation x1, loops' own time, lower_inverse(): return jax.scipy.linalg.solve_triangular(lower, identity, lower=True)  12.4 us
  transfers between devices with their start and end apart: 2, of which 2 were waited for; matrix products, arithmetic and copies ran while one was open for 0% of the time, Pallas kernels for 0%

profile of v1, /device:TPU:1, one launch (start us, length us, event | category | flops | bytes accessed | tf_op | source)
XLA Modules:
  0.0 478.2 jit_solution(4305613524410411497)
XLA Ops:
  7.2 1.5 copy-done
  8.8 4.2 fusion.14
  13.4 144.8 %all-reduce.4.cloned.1.call-done = f32[256,256]{0,1:T(8,128)} async-done(((f32[256,256]{0,1:T(8,128)}), f32[256,256]{0,1:T(8,128)}) %all-reduce.4.cloned.1.call-update) | async-done | bytes 262160 | tf_op jit(solution)/shard_map/psum | solution.py:24
  158.2 1.1 copy.6
  159.3 1.0 fusion.3
  160.3 11.7 %cholesky.50 = f32[128,128]{1,0:T(8,128)S(1)} custom-call(f32[128,128]{1,0:T(8,128)S(1)} %cholesky.118), custom_call_target="Cholesky" | custom-call | tf_op jit(solution)/shard_map/jit(cholesky)/cholesky | solution.py:13
  172.0 9.8 %custom-call.15 = f32[1,128,128]{1,2,0:T(8,128)S(1)} custom-call(f32[1,128,128]{2,1,0:T(8,128)S(1)} %get-tuple-element.29), custom_call_target="InvertDiagBlocksLowerTriangular" | custom-call | tf_op jit(solution)/shard_map/jit(cholesky)/cholesky | solution.py:13
  182.3 11.7 %cholesky.105 = f32[128,128]{1,0:T(8,128)S(1)} custom-call(f32[128,128]{1,0:T(8,128)S(1)} %convolution_subtract_fusion.2), custom_call_target="Cholesky" | custom-call | tf_op jit(solution)/shard_map/jit(cholesky)/cholesky | solution.py:13
  194.1 0.6 compare_reduce_fusion
  196.2 16.3 %while.1 = (s32[]{:T(128)}, f32[256,256]{1,0:T(8,128)S(1)}, s32[2,2]{1,0:T(2,128)S(1)}, f32[2,128,128]{2,1,0:T(8,128)S(1)}, s32[]{:T(128)}) while((s32[]{:T(128)}, f32[256,256]{1,0:T(8,128)S(1)}, s32[2,2]{1,0:T(2,128)S(1)}, f32[2,128,128]{2,1,0:T(8,128)S(1)}, s32[]{:T(128)}) %tuple.29), condition=%wide.while_cond, body=%wide.while_body.sunk | while | flops 2 | bytes 131189 | solution.py:18
  208.5 0.6 fusion.28
  209.1 1.4 bitcast_dynamic-update-slice_fusion.2
  211.1 1.4 bitcast_dynamic-update-slice_fusion.2
  212.5 19.7 %custom-call.16 = f32[2,128,128]{1,2,0:T(8,128)S(1)} custom-call(f32[2,128,128]{2,1,0:T(8,128)S(1)} %get-tuple-element.10), custom_call_target="InvertDiagBlocksLowerTriangular" | custom-call | tf_op jit(solution)/shard_map/jit(_solve_triangular)/triangular_solve | solution.py:18
  233.0 3.3 convolution_bitcast_fusion
  236.3 2.9 copy.7
  239.2 2.4 stack.2
  241.6 96.6 %all_to_all.5 = f32[4,2048,256]{2,1,0:T(8,128)S(1)} all-to-all(f32[4,2048,256]{2,1,0:T(8,128)S(1)} %stack.2), channel_id=1, replica_groups=mesh['rows'=32,'cols'=4] {'cols'}, dimensions={0} | all-to-all | bytes 16777216 | tf_op jit(solution)/shard_map/all_to_all | solution.py:29
  338.2 3.2 copy-done.1
  341.4 14.7 %fusion.15 = f32[256,256]{1,0:T(8,128)} fusion(f32[8192,256]{1,0:T(8,128)S(1)} %bitcast.43, f32[8192,256]{1,0:T(8,128)S(1)} %bitcast.46), kind=kOutput, calls=%fused_computation.39 | convolution fusion | flops 6442450944 | bytes 17039360 | tf_op jit(solution)/shard_map/dot_general | solution.py:9
  356.2 0.8 copy.8
  357.0 98.9 %all-reduce.6.cloned.1.call-done = f32[256,256]{1,0:T(8,128)} async-done(((f32[256,256]{1,0:T(8,128)}), f32[256,256]{1,0:T(8,128)}) %all-reduce.6.cloned.1.call-update) | async-done | bytes 262160 | tf_op jit(solution)/shard_map/psum | solution.py:31
  455.9 14.5 %convolution_subtract_fusion = f32[8192,256]{1,0:T(8,128)} fusion(f32[8192,256]{1,0:T(8,128)} %param.3, f32[8192,256]{1,0:T(8,128)} %bitcast.44, f32[256,256]{1,0:T(8,128)} %all-reduce.6.cloned.1.call-done), kind=kOutput, calls=%fused_computation.2 | convolution fusion | flops 6444548096 | bytes 25427968 | tf_op jit(solution)/shard_map/dot_general | solution.py:9
  470.4 0.7 broadcast_multiply_fusion
  (30 shorter events, 2.7 us)
Async XLA Ops:
  7.2 1.6 copy-start
  7.2 151.0 %all-reduce.4.cloned.1.call-start = ((), (), s32[]{:S(2)}) async-start(), calls=%async_computation.1 | async-start | bytes 524288 | tf_op jit(solution)/shard_map/psum | solution.py:24
  12.9 442.9 %all-reduce.6.cloned.1.call-start = ((), (), s32[]{:S(2)}) async-start(), calls=%async_computation.2 | async-start | bytes 524288 | tf_op jit(solution)/shard_map/psum | solution.py:31
  239.2 102.2 %slice-start = ((s8[8388608]{0:T(1024)(128)(4,1)}), s8[4194304]{0:T(1024)(128)(4,1)S(1)}, s32[]{:S(2)}) async-start(s8[8388608]{0:T(1024)(128)(4,1)} %bitcast.45), calls=%async_computation.3 | async-start | bytes 8388608
  241.6 99.8 %slice-start.1 = ((s8[8388608]{0:T(1024)(128)(4,1)}), s8[4194304]{0:T(1024)(128)(4,1)S(1)}, s32[]{:S(2)}) async-start(s8[8388608]{0:T(1024)(128)(4,1)} %bitcast.45), calls=%async_computation.4 | async-start | bytes 8388608
  338.2 3.2 copy-start.1
  455.9 14.5 %copy-start.2 = (f32[256,256]{1,0:T(8,128)S(1)}, f32[256,256]{1,0:T(8,128)}, u32[]{:S(2)}) copy-start(f32[256,256]{1,0:T(8,128)} %all-reduce.6.cloned.1.call-done) | copy-start | bytes 786436
Sparse Core Ops, SparseCore 0:
  13.3 144.8 all-reduce.3
  356.3 99.5 all-reduce.5

commit v2 on v0

--- a/solution.py
+++ b/solution.py
@@ -26,7 +26,7 @@
     inverse = lower_inverse(lower)
     basis_part = matmul(panel_cols, inverse.T)
     orthonormal = lax.all_gather(basis_part, "cols", axis=0, tiled=True)
-    coupling = lax.psum(matmul(orthonormal.T, trailing), "rows")
+    coupling = jnp.sum(lax.all_gather(matmul(orthonormal.T, trailing), "rows"), axis=0)
     updated = trailing - matmul(orthonormal, coupling)
     return (lower.T * shrink, coupling * shrink, updated)
 

time: 447 us -> 401 us (0.90)
  waiting for transfers between devices: 327 us -> 279 us
    psum x1 -> x0, waiting for transfers between devices: 102 us -> none  [local(): coupling = lax.psum(matmul(orthonormal.T, trailing), 'rows')]
    all_gather x0 -> x1, waiting for transfers between devices: none -> 53.7 us  [local(): lax.all_gather(matmul(orthonormal.T, trailing), 'rows')]
where the time goes in v2:
time: 401 us
  waiting for transfers between devices  279 us (70%)
  other arithmetic  59.3 us (15%)
  matrix products  39 us (10%)
  between operations  15.2 us (4%)
  local copies, waits for them, and re-layouts  7.5 us (2%)
    psum x1, waiting for transfers between devices, local(): gram_sum = lax.psum(matmul(panel_cols.T, panel_cols), ('rows', 'cols'))  145 us
    all_gather x1, waiting for transfers between devices, local(): orthonormal = lax.all_gather(basis_part, 'cols', axis=0, tiled=True)  80.6 us
    all_gather x1, waiting for transfers between devices, local(): lax.all_gather(matmul(orthonormal.T, trailing), 'rows')  53.7 us
    dot_general x4, matrix products, matmul(): return jnp.dot(left, right, precision=lax.Precision.HIGHEST)  37.7 us
    another operation x6, other arithmetic, lower_factor(): return jnp.linalg.cholesky(gram_sum)  34 us
    another operation x3, other arithmetic, lower_inverse(): return jax.scipy.linalg.solve_triangular(lower, identity, lower=True)  19.7 us
  transfers between devices with their start and end apart: 3, of which 3 were waited for; matrix products, arithmetic and copies ran while one was open for 0% of the time, Pallas kernels for 0%

profile of v2, /device:TPU:1, one launch (start us, length us, event | category | flops | bytes accessed | tf_op | source)
XLA Modules:
  0.0 400.9 jit_solution(11327719766925225595)
XLA Ops:
  7.2 1.5 copy-done
  8.8 4.2 %fusion.14 = f32[256,256]{0,1:T(8,128)} fusion(f32[2048,256]{1,0:T(8,128)S(1)} %copy-done), kind=kOutput, calls=%fused_computation.38 | convolution fusion | flops 1610612736 | bytes 2359296 | tf_op jit(solution)/shard_map/dot_general | solution.py:9
  13.2 144.9 %all-reduce.3.cloned.1.call-done = f32[256,256]{0,1:T(8,128)} async-done(((f32[256,256]{0,1:T(8,128)}), f32[256,256]{0,1:T(8,128)}) %all-reduce.3.cloned.1.call-update) | async-done | bytes 262160 | tf_op jit(solution)/shard_map/psum | solution.py:24
  158.2 1.1 copy.6
  159.2 1.0 fusion.3
  160.2 11.7 %cholesky.50 = f32[128,128]{1,0:T(8,128)S(1)} custom-call(f32[128,128]{1,0:T(8,128)S(1)} %cholesky.118), custom_call_target="Cholesky" | custom-call | tf_op jit(solution)/shard_map/jit(cholesky)/cholesky | solution.py:13
  172.0 9.8 %custom-call.15 = f32[1,128,128]{1,2,0:T(8,128)S(1)} custom-call(f32[1,128,128]{2,1,0:T(8,128)S(1)} %get-tuple-element.29), custom_call_target="InvertDiagBlocksLowerTriangular" | custom-call | tf_op jit(solution)/shard_map/jit(cholesky)/cholesky | solution.py:13
  182.3 11.7 %cholesky.105 = f32[128,128]{1,0:T(8,128)S(1)} custom-call(f32[128,128]{1,0:T(8,128)S(1)} %convolution_subtract_fusion.2), custom_call_target="Cholesky" | custom-call | tf_op jit(solution)/shard_map/jit(cholesky)/cholesky | solution.py:13
  194.1 0.6 compare_reduce_fusion
  196.1 4.2 %while.1 = (s32[]{:T(128)}, f32[256,256]{1,0:T(8,128)S(1)}, s32[2,2]{1,0:T(2,128)S(1)}, f32[2,128,128]{2,1,0:T(8,128)S(1)}, s32[]{:T(128)}) while((s32[]{:T(128)}, f32[256,256]{1,0:T(8,128)S(1)}, s32[2,2]{1,0:T(2,128)S(1)}, f32[2,128,128]{2,1,0:T(8,128)S(1)}, s32[]{:T(128)}) %tuple.29), condition=%wide.while_cond, body=%wide.while_body.sunk | while | flops 2 | bytes 131189 | solution.py:18
  196.3 0.6 fusion.28
  196.9 1.4 bitcast_dynamic-update-slice_fusion.2
  198.3 0.6 fusion.28
  198.9 1.4 bitcast_dynamic-update-slice_fusion.2
  200.3 19.7 %custom-call.16 = f32[2,128,128]{1,2,0:T(8,128)S(1)} custom-call(f32[2,128,128]{2,1,0:T(8,128)S(1)} %get-tuple-element.10), custom_call_target="InvertDiagBlocksLowerTriangular" | custom-call | tf_op jit(solution)/shard_map/jit(_solve_triangular)/triangular_solve | solution.py:18
  220.5 0.3 fusion.8
  220.8 3.3 convolution_bitcast_fusion
  224.2 80.6 %all-gather.4.cloned.1.call-done = f32[8192,256]{0,1:T(8,128)} async-done(((f32[2048,256]{0,1:T(8,128)}), f32[8192,256]{0,1:T(8,128)}) %all-gather.4.cloned.1.call-update) | async-done | bytes 8388624 | tf_op jit(solution)/shard_map/all_gather | solution.py:28
  304.8 11.4 %fusion.15 = f32[256,256]{1,0:T(8,128)} fusion(f32[8192,256]{0,1:T(8,128)} %all-gather.4.cloned.1.call-done, f32[8192,256]{1,0:T(8,128)} %param.3), kind=kOutput, calls=%fused_computation.39 | convolution fusion | flops 6442450944 | bytes 17039360 | tf_op jit(solution)/shard_map/dot_general | solution.py:9
  316.2 0.8 copy.7
  317.1 53.7 %all-gather.6.cloned.1.call-done = f32[8192,256]{1,0:T(8,128)} async-done(((f32[256,256]{1,0:T(8,128)}), f32[8192,256]{1,0:T(8,128)}) %all-gather.6.cloned.1.call-update) | async-done | bytes 8388624 | tf_op jit(solution)/shard_map/all_gather | solution.py:29
  370.8 3.9 reduce_sum.9
  374.7 0.7 broadcast_multiply_fusion
  375.5 18.9 %convolution_subtract_fusion = f32[8192,256]{1,0:T(8,128)} fusion(f32[8192,256]{1,0:T(8,128)} %param.3, f32[8192,256]{0,1:T(8,128)} %all-gather.4.cloned.1.call-done, f32[256,256]{1,0:T(8,128)S(1)} %reduce_sum.9), kind=kOutput, calls=%fused_computation.2 | convolution fusion | flops 6444548096 | bytes 25427968 | tf_op jit(solution)/shard_map/dot_general | solution.py:9
  (22 shorter events, 1.6 us)
Async XLA Ops:
  7.2 1.6 copy-start
  7.2 151.0 %all-reduce.3.cloned.1.call-start = ((), (), s32[]{:S(2)}) async-start(), calls=%async_computation | async-start | bytes 524288 | tf_op jit(solution)/shard_map/psum | solution.py:24
  12.9 291.9 %all-gather.4.cloned.1.call-start = ((), (), s32[]{:S(2)}) async-start(), calls=%async_computation.1 | async-start | bytes 10485760 | tf_op jit(solution)/shard_map/all_gather | solution.py:28
  224.1 146.7 %all-gather.6.cloned.1.call-start = ((), (), s32[]{:S(2)}) async-start(), calls=%async_computation.2 | async-start | bytes 8650752 | tf_op jit(solution)/shard_map/all_gather | solution.py:29
Sparse Core Ops, SparseCore 0:
  13.3 144.7 all-reduce.2
  224.3 80.5 all-gather.3
  316.3 54.4 all-gather.5
